TPU v7x, 32 devices: a whole 2x2x4 slice. The times are simulated.
32 devices in a mesh: row: 4 (over z), col: 8 (over y, x, core).
Axes of the slice: x: 2, y: 2, z: 4, core: 2. Of those that a mesh axis runs over, the one named last changes fastest.
Arguments:
- pretrained_weight: bfloat16 [4096, 53248], P('row', 'col'), may hold values from -45 to 45, as said below
- up_factors: bfloat16 [4096, 2048], P('row', 'col'), may hold values from -0.125 to 0.125
- down_factors: bfloat16 [2048, 53248], P('row', 'col'), may hold values from -6 to 6
- adapter_weights: float32 [32], replicated, may hold values from 0.2 to 1.5
Outputs:
- quantized: bfloat16 [4096, 53248], P(None, ('col', 'row'))
- block_scale: float32 [32, 416], P('row', 'col')
Inputs may be any that keep to these rules, and one draw needn't show every extreme that they name: `pretrained_weight`: entries of varied scale from row to row and column to column.
All inputs are finite; a program needn't handle non-finite values. Where the computation divides by a largest or mean magnitude, that divisor is 1e-20 or more.
Results may differ from a plain program's by a relative error of at most 0.0028.
Values may be sent and summed in bfloat16 or wider, within the bound.
A program may use at most 192 MiB of HBM per device.

v0:
```python
import jax
import jax.numpy as jnp
from jax import lax
from jax.sharding import PartitionSpec as P

RANK = 64
QB = 128


def scale_tiles(merged_weight):
    row_count, col_count = merged_weight.shape
    tiles = merged_weight.reshape(row_count // QB, QB, col_count // QB, QB)
    largest = jnp.max(jnp.abs(tiles), axis=(1, 3)) + 1e-06
    values = (tiles / largest[:, None, :, None]).astype(jnp.bfloat16).reshape(row_count, col_count)
    return (values, largest)


def shards(pretrained_weight, up_factors, down_factors, adapter_weights):
    local_rank_slab = up_factors.shape[1]
    broadcast_scales = jnp.repeat(adapter_weights, RANK)
    offset = lax.axis_index("col") * local_rank_slab
    local_scale = lax.dynamic_slice_in_dim(broadcast_scales, offset, local_rank_slab, 0)
    weighted_update = (up_factors.astype(jnp.float32) * local_scale[None, :]).astype(jnp.bfloat16)
    b_panel = lax.all_gather(weighted_update, "col", axis=1, tiled=True)
    merged_weight = pretrained_weight.astype(jnp.float32) + jnp.dot(
        b_panel,
        lax.all_gather(down_factors, "row", axis=0, tiled=True),
        preferred_element_type=jnp.float32,
    )
    values, largest = scale_tiles(merged_weight)
    serving = lax.all_to_all(values, "row", split_axis=1, concat_axis=0, tiled=True)
    return (serving, largest)


def solution(mesh):
    return jax.shard_map(
        shards,
        mesh=mesh,
        in_specs=(P("row", "col"), P("row", "col"), P("row", "col"), P()),
        out_specs=(P(None, ("col", "row")), P("row", "col")),
        check_vma=False,
    )
```

profile of v0, /device:TPU:0, one launch (start us, length us, event | category | flops | bytes accessed | tf_op | source)
XLA Modules:
  0.0 1016.4 jit_solution(8588907456522843669)
XLA Ops:
  7.2 0.0 all-gather.3.cloned.1.call-start
  7.2 0.7 broadcast_in_dim.2
  7.9 0.1 reshape.18
  8.0 0.1 dynamic_slice.3
  8.1 1.9 multiply_convert_fusion
  10.0 0.0 all-gather.3.cloned.1.call-update
  10.0 0.0 all-gather.5.cloned.1.call-start
  10.1 0.7 all-gather.5.cloned.1.call-update
  10.8 39.8 %all-gather.3.cloned.1.call-done = bf16[1024,2048]{1,0:T(8,128)(2,1)} async-done(((bf16[1024,256]{1,0:T(8,128)(2,1)}), bf16[1024,2048]{1,0:T(8,128)(2,1)}) %all-gather.3.cloned.1.call-update) | async-done | bytes 4194320 | tf_op jit(solution)/shard_map/all_gather | solution.py:24
  50.6 460.8 %all-gather.5.cloned.1.call-done = bf16[2048,6656]{1,0:T(8,128)(2,1)} async-done(((bf16[512,6656]{1,0:T(8,128)(2,1)}), bf16[2048,6656]{1,0:T(8,128)(2,1)}) %all-gather.5.cloned.1.call-update) | async-done | bytes 27262992 | tf_op jit(solution)/shard_map/all_gather | solution.py:27
  511.4 42.3 %fusion = (f32[1024,6656]{1,0:T(8,128)}, f32[1024,6656]{1,0:T(8,128)}) fusion(bf16[1024,6656]{1,0:T(8,128)(2,1)} %param.4, bf16[1024,2048]{1,0:T(8,128)(2,1)} %all-gather.3.cloned.1.call-done, bf16[2048,6656]{1,0:T(8,128)(2,1)} %all-gather.5.cloned.1.call-done), kind=kOutput, calls=%fused_computation.3 | convolution fusion | flops 27937734656 | bytes 99614720 | tf_op jit(solution)/shard_map/dot_general | solution.py:25
  553.7 29.6 %reshape.19 = f32[8,128,52,128]{3,2,1,0:T(8,128)} reshape(f32[1024,6656]{1,0:T(8,128)} %get-tuple-element.4) | data formatting | bytes 54525952 | tf_op jit(solution)/shard_map/abs | solution.py:13
  583.3 11.3 %reduce_max.9 = f32[8,52]{1,0:T(8,128)S(1)} reduce(f32[8,128,52,128]{3,2,1,0:T(8,128)} %reshape.19, f32[]{:T(128)} %constant.4.clone.1), dimensions={1,3}, to_apply=%region_0.0 | reduce | flops 6815328 | bytes 27264644 | tf_op jit(solution)/shard_map/reduce_max | solution.py:13
  594.6 0.1 copy.16
  594.7 10.8 %div.11 = f32[8,128,52,128]{1,0,3,2:T(8,128)} broadcast(f32[8,52]{0,1:T(8,128)S(1)} %broadcast_add_fusion), dimensions={0,2} | broadcast | bytes 27264640 | tf_op jit(solution)/shard_map/div | solution.py:14
  605.5 24.8 %copy.21 = f32[832,8,8,128]{3,1,2,0:T(8,128)} copy(f32[832,8,8,128]{3,2,1,0:T(8,128)} %bitcast.17) | data formatting | bytes 54525952
  630.4 25.6 %copy.12 = f32[1024,6656]{1,0:T(8,128)} copy(f32[1024,6656]{0,1:T(8,128)} %bitcast.16) | data formatting | bytes 54525952 | tf_op jit(solution)/shard_map/div | solution.py:14
  655.9 26.6 %divide_convert_fusion = bf16[1024,6656]{1,0:T(8,128)(2,1)} fusion(f32[1024,6656]{1,0:T(8,128)} %copy.12, f32[1024,6656]{1,0:T(8,128)} %get-tuple-element.5, bf16[1024,6656]{1,0:T(8,128)(2,1)} %param.4), kind=kLoop, calls=%fused_computation.1 | loop fusion | flops 27262976 | bytes 81788928 | tf_op jit(solution)/shard_map/convert_element_type | solution.py:14
  682.5 12.2 %copy.22 = bf16[128,4,8,1664]{3,2,0,1:T(8,128)(2,1)} copy(bf16[128,4,8,1664]{3,2,1,0:T(8,128)(2,1)} %bitcast.18) | data formatting | bytes 27262976 | tf_op jit(solution)/shard_map/all_to_all | solution.py:31
  694.7 6.5 all-to-all-start
  701.2 0.7 copy.14
  701.8 295.3 %all-to-all-done = bf16[1024,4,1664]{2,0,1:T(8,128)(2,1)} async-done(((bf16[1024,4,1664]{2,0,1:T(8,128)(2,1)}), bf16[1024,4,1664]{2,0,1:T(8,128)(2,1)}, u32[]{:S(2)}, u32[]{:S(2)}) %all-to-all-start) | async-done | bytes 13631520 | tf_op jit(solution)/shard_map/all_to_all | solution.py:31
  997.1 12.4 %copy.24 = bf16[4096,1664]{1,0:T(8,128)(2,1)} copy(bf16[4096,1664]{1,0:T(8,128)(2,1)} %bitcast.1) | data formatting | bytes 27262976
  (1 shorter events, 0.0 us)
Async XLA Ops:
  7.2 43.5 %all-gather.3.cloned.1.call-start = ((), (), s32[]{:S(2)}) async-start(), calls=%async_computation.1 | async-start | bytes 4718592 | tf_op jit(solution)/shard_map/all_gather | solution.py:24
  10.0 501.3 %all-gather.5.cloned.1.call-start = ((), (), s32[]{:S(2)}) async-start(), calls=%async_computation.2 | async-start | bytes 34078720 | tf_op jit(solution)/shard_map/all_gather | solution.py:27
  694.7 302.4 %all-to-all-start = ((bf16[1024,4,1664]{2,0,1:T(8,128)(2,1)}), bf16[1024,4,1664]{2,0,1:T(8,128)(2,1)}, u32[]{:S(2)}, u32[]{:S(2)}) async-start(bf16[1024,4,1664]{2,0,1:T(8,128)(2,1)} %bitcast.19), calls=%async_computation | async-start | bytes 27262976 | tf_op jit(solution)/shard_map/all_to_all | solution.py:31
Sparse Core Ops, SparseCore 0:
  10.4 40.1 all-gather.2
  52.2 459.1 all-gather.4
where the time goes:
time: 1020 us
  waiting for transfers between devices  797 us (78%)
  local copies, waits for them, and re-layouts  117 us (11%)
  matrix products  42.3 us (4%)
  other arithmetic  39.8 us (4%)
  between operations  14.1 us (1%)
    all_gather x1, waiting for transfers between devices, shards(): lax.all_gather(down_factors, 'row', axis=0, tiled=True)  461 us
    all_to_all x1, waiting for transfers between devices, shards(): lax.all_to_all(values, 'row', split_axis=1, concat_axis=0, tiled=True)  295 us
    dot_general x1, matrix products, shards(): jnp.dot(b_panel, lax.all_gather(down_factors, 'row', axis=0, tiled=True),...  42.3 us
    all_gather x1, waiting for transfers between devices, shards(): b_panel = lax.all_gather(weighted_update, 'col', axis=1, tiled=True)  39.8 us
    unnamed x4, local copies, waits for them, and re-layouts  38 us
    div x2, local copies, waits for them, and re-layouts, scale_tiles(): tiles / largest[:, None, :, None]  36.4 us
    abs x1, local copies, waits for them, and re-layouts, scale_tiles(): largest = jnp.max(jnp.abs(tiles), axis=(1, 3)) + 1e-06  29.6 us
    convert_element_type x1, other arithmetic, scale_tiles(): (tiles / largest[:, None, :, None]).astype(jnp.bfloat16)  26.6 us
  transfers between devices with their start and end apart: 3, of which 3 were waited for; matrix products, arithmetic and copies ran while one was open for 0% of the time, Pallas kernels for 0%

commit v1 on v0

v1 whole, which is shorter than its diff:
```python
import functools

import jax
import jax.numpy as jnp
from jax import lax
from jax.experimental import pallas as pl
from jax.experimental.pallas import tpu as pltpu
from jax.sharding import PartitionSpec as P

RANK = 64
QB = 128
CHUNK = 256


def weighted_factors(up_factors, adapter_weights):
    local_rank_slab = up_factors.shape[1]
    broadcast_scales = jnp.repeat(adapter_weights, RANK)
    offset = lax.axis_index("col") * local_rank_slab
    local_scale = lax.dynamic_slice_in_dim(broadcast_scales, offset, local_rank_slab, 0)
    return (up_factors.astype(jnp.float32) * local_scale[None, :]).astype(jnp.bfloat16)


def scale_tiles(merged_weight):
    row_count, col_count = merged_weight.shape
    tiles = merged_weight.reshape(row_count // QB, QB, col_count // QB, QB)
    largest = jnp.max(jnp.abs(tiles), axis=(1, 3)) + 1e-06
    values = (tiles / largest[:, None, :, None]).astype(jnp.bfloat16).reshape(row_count, col_count)
    return (values, largest)


def panel_shards(pretrained_weight, up_factors, down_factors, adapter_weights):
    weighted_update = weighted_factors(up_factors, adapter_weights)
    b_panel = lax.all_gather(weighted_update, "col", axis=1, tiled=True)
    merged_weight = pretrained_weight.astype(jnp.float32) + jnp.dot(
        b_panel,
        lax.all_gather(down_factors, "row", axis=0, tiled=True),
        preferred_element_type=jnp.float32,
    )
    values, largest = scale_tiles(merged_weight)
    serving = lax.all_to_all(values, "row", split_axis=1, concat_axis=0, tiled=True)
    return (serving, largest)


def merge_kernel(
    nr, nc, b_in, a_in, w_in, out, scales_out,
    a_full, b_full, w_full, o_buf, s_own, s_all,
    a_send, a_recv, b_send, b_recv, w_send, w_recv, s_send, s_recv, o_sem, local_sem,
):
    rows, width = w_in.shape
    cols = width // nr
    depth = a_in.shape[0]
    planes = nc // 2
    chunks = rows // CHUNK
    per_chunk = CHUNK // QB
    blocks = cols // QB
    r = lax.axis_index("row")
    c = lax.axis_index("col")
    chip, core = c // 2, lax.rem(c, 2)
    sibling = chip * 2 + (1 - core)

    def z_peer(i):
        return lax.rem(r + i, nr)

    def plane_peer(i):
        return lax.rem(chip + i, planes) * 2 + core

    barrier = pltpu.get_barrier_semaphore()
    for i in range(1, nr):
        pl.semaphore_signal(barrier, inc=1, device_id={"row": z_peer(i)}, device_id_type=pl.DeviceIdType.MESH)
    for i in range(1, planes):
        pl.semaphore_signal(barrier, inc=1, device_id={"col": plane_peer(i)}, device_id_type=pl.DeviceIdType.MESH)
    pl.semaphore_signal(barrier, inc=1, device_id={"col": sibling}, device_id_type=pl.DeviceIdType.MESH)
    pl.semaphore_wait(barrier, nr - 1 + planes - 1 + 1)

    def columns(j):
        return pl.ds(pl.multiple_of(j * cols, QB), cols)

    def b_z(i, src, slot):
        return pltpu.make_async_remote_copy(
            src_ref=src, dst_ref=b_full.at[slot[1], pl.ds(slot[0] * rows, rows), :],
            send_sem=b_send.at[0, i], recv_sem=b_recv.at[slot[0], slot[1]],
            device_id={"row": z_peer(i)}, device_id_type=pl.DeviceIdType.MESH)

    def b_slot(j, q):
        return b_full.at[q, pl.ds(j * rows, rows), :]

    for i in range(1, nr):
        pltpu.make_async_remote_copy(
            src_ref=b_in, dst_ref=b_slot(r, c), send_sem=b_send.at[0, i], recv_sem=b_recv.at[r, c],
            device_id={"row": z_peer(i)}, device_id_type=pl.DeviceIdType.MESH).start()
    for i in range(1, nr):
        pltpu.make_async_remote_copy(
            src_ref=a_in.at[:, columns(z_peer(i))], dst_ref=a_full.at[pl.ds(r * depth, depth), :],
            send_sem=a_send.at[i], recv_sem=a_recv.at[r],
            device_id={"row": z_peer(i)}, device_id_type=pl.DeviceIdType.MESH).start()
    own_a = pltpu.make_async_copy(a_in.at[:, columns(r)], a_full.at[pl.ds(r * depth, depth), :], local_sem.at[0])
    own_a.start()
    own_b = pltpu.make_async_copy(b_in, b_slot(r, c), local_sem.at[1])
    own_b.start()
    own_w = pltpu.make_async_copy(w_in.at[:, columns(r)], w_full.at[pl.ds(r * rows, rows), :], local_sem.at[2])
    own_w.start()

    def w_copy(i, t):
        source = pl.multiple_of(t * CHUNK, CHUNK)
        return pltpu.make_async_remote_copy(
            src_ref=w_in.at[pl.ds(source, CHUNK), columns(z_peer(i))],
            dst_ref=w_full.at[pl.ds(pl.multiple_of(r * rows + t * CHUNK, CHUNK), CHUNK), :],
            send_sem=w_send.at[i, t], recv_sem=w_recv.at[r, t],
            device_id={"row": z_peer(i)}, device_id_type=pl.DeviceIdType.MESH)

    @pl.loop(0, chunks)
    def _(t):
        for i in range(1, nr):
            w_copy(i, t).start()

    def b_wait(j, q):
        slot = b_slot(j, q)
        pltpu.make_async_copy(slot, slot, b_recv.at[j, q]).wait()

    def b_share(k, j, q, to, src):
        return pltpu.make_async_remote_copy(
            src_ref=src, dst_ref=b_slot(j, q), send_sem=b_send.at[1 + k[0], k[1]], recv_sem=b_recv.at[j, q],
            device_id={"col": to}, device_id_type=pl.DeviceIdType.MESH)

    own_b.wait()

    def spread(m, j):
        for i in range(1, planes):
            b_share((m, i), j, c, plane_peer(i), b_slot(j, c)).start()
        b_share((m, planes), j, c, sibling, b_slot(j, c)).start()

    spread(0, r)
    for m in range(1, nr):
        j = z_peer(m)
        b_wait(j, c)
        spread(m, j)
    for m in range(nr):
        j = z_peer(m)
        for i in range(1, planes):
            q = plane_peer(i)
            b_wait(j, q)
            b_share((m, planes + i), j, q, sibling, b_slot(j, q)).start()
    for m in range(nr):
        j = z_peer(m)
        for i in range(planes):
            b_wait(j, lax.rem(chip + i, planes) * 2 + (1 - core))

    own_a.wait()
    for i in range(1, nr):
        part = a_full.at[pl.ds(z_peer(i) * depth, depth), :]
        pltpu.make_async_copy(part, part, a_recv.at[z_peer(i)]).wait()

    def merge_cols(slot, j, t, col, count):
        row = pl.multiple_of(j * rows + t * CHUNK, CHUNK)
        at = pl.ds(row, CHUNK)
        lhs = jnp.concatenate([b_full[q, at, :] for q in range(nc)], axis=1)
        part = pl.ds(pl.multiple_of(col * QB, QB), count * QB)
        merged = w_full[at, part].astype(jnp.float32) + jnp.dot(
            lhs, a_full[:, part], preferred_element_type=jnp.float32)
        for y in range(per_chunk):
            for x in range(count):
                tile = merged[y * QB:(y + 1) * QB, x * QB:(x + 1) * QB]
                largest = jnp.max(jnp.max(jnp.abs(tile), axis=0, keepdims=True), axis=1, keepdims=True) + 1e-06
                o_buf[slot, y * QB:(y + 1) * QB, pl.ds(pl.multiple_of((col + x) * QB, QB), QB)] = (
                    tile / largest).astype(jnp.bfloat16)
                s_own[j, t * per_chunk + y, pl.ds(col + x, 1), :] = jnp.broadcast_to(largest, (1, QB))

    def o_copy(slot, j, t):
        return pltpu.make_async_copy(
            o_buf.at[slot], out.at[pl.ds(pl.multiple_of(j * rows + t * CHUNK, CHUNK), CHUNK), :], o_sem.at[slot])

    def merge_chunk(n, j, t):
        slot = lax.rem(n, 2)

        @pl.when(n >= 2)
        def _():
            o_copy(slot, j, t).wait()

        @pl.loop(0, blocks // 2)
        def _(pair):
            merge_cols(slot, j, t, pair * 2, 2)

        if blocks % 2:
            merge_cols(slot, j, t, blocks - 1, 1)
        o_copy(slot, j, t).start()

    own_w.wait()

    @pl.loop(0, chunks)
    def _(t):
        merge_chunk(t, r, t)

    @pl.loop(0, chunks * (nr - 1))
    def _(n):
        t = n // (nr - 1)
        j = lax.rem(r + 1 + lax.rem(n, nr - 1), nr)
        part = w_full.at[pl.ds(pl.multiple_of(j * rows + t * CHUNK, CHUNK), CHUNK), :]
        pltpu.make_async_copy(part, part, w_recv.at[j, t]).wait()
        merge_chunk(n + chunks, j, t)

    def s_copy(i):
        return pltpu.make_async_remote_copy(
            src_ref=s_own.at[z_peer(i)], dst_ref=s_all.at[r], send_sem=s_send.at[i], recv_sem=s_recv.at[r],
            device_id={"row": z_peer(i)}, device_id_type=pl.DeviceIdType.MESH)

    for i in range(1, nr):
        s_copy(i).start()
    s_all[r] = s_own[r]
    for slot in range(2):
        o_copy(slot, r, slot).wait()
    for i in range(1, nr):
        pltpu.make_async_copy(s_own.at[0], s_all.at[z_peer(i)], s_recv.at[z_peer(i)]).wait()
    to_out = pltpu.make_async_copy(s_all, scales_out, local_sem.at[3])
    to_out.start()

    for i in range(1, nr):
        s_copy(i).wait_send()
        pltpu.make_async_copy(b_in, b_in, b_send.at[0, i]).wait()
        part = a_full.at[pl.ds(r * depth, depth), :]
        pltpu.make_async_copy(part, part, a_send.at[i]).wait()
    for m in range(nr):
        for k in range(1, 2 * planes):
            pltpu.make_async_copy(b_in, b_in, b_send.at[1 + m, k]).wait()

    @pl.loop(0, chunks)
    def _(t):
        for i in range(1, nr):
            w_copy(i, t).wait_send()

    to_out.wait()


def merge(nr, nc, b, a, w):
    rows, width = w.shape
    cols = width // nr
    depth = a.shape[0]
    chunks = rows // CHUNK
    blocks = cols // QB
    dma = pltpu.SemaphoreType.DMA
    return pl.pallas_call(
        functools.partial(merge_kernel, nr, nc),
        out_shape=[
            jax.ShapeDtypeStruct((nr * rows, cols), jnp.bfloat16),
            jax.ShapeDtypeStruct((nr, rows // QB, blocks, QB), jnp.float32),
        ],
        in_specs=[pl.BlockSpec(memory_space=pl.ANY)] * 3,
        out_specs=[pl.BlockSpec(memory_space=pl.ANY)] * 2,
        scratch_shapes=[
            pltpu.VMEM((nr * depth, cols), jnp.bfloat16),
            pltpu.VMEM((nc, nr * rows, b.shape[1]), jnp.bfloat16),
            pltpu.VMEM((nr * rows, cols), jnp.bfloat16),
            pltpu.VMEM((2, CHUNK, cols), jnp.bfloat16),
            pltpu.VMEM((nr, rows // QB, blocks, QB), jnp.float32),
            pltpu.VMEM((nr, rows // QB, blocks, QB), jnp.float32),
            dma((nr,)), dma((nr,)),
            dma((nr + 1, nc)), dma((nr, nc)),
            dma((nr, chunks)), dma((nr, chunks)),
            dma((nr,)), dma((nr,)),
            dma((2,)), dma((4,)),
        ],
        compiler_params=pltpu.CompilerParams(
            collective_id=0, has_side_effects=True, vmem_limit_bytes=60 * 2 ** 20),
        cost_estimate=pl.CostEstimate(
            flops=2 * nr * rows * nr * depth * cols, bytes_accessed=4 * rows * width, transcendentals=0),
    )(b, a, w)


def serving_shards(nr, nc, pretrained_weight, up_factors, down_factors, adapter_weights):
    weighted_update = weighted_factors(up_factors, adapter_weights)
    values, scales = merge(nr, nc, weighted_update, down_factors, pretrained_weight)
    largest = jnp.transpose(scales[:, :, :, 0], (1, 0, 2)).reshape(scales.shape[1], -1)
    return (values, largest)


def solution(mesh):
    nr, nc = mesh.shape["row"], mesh.shape["col"]

    def shards(pretrained_weight, up_factors, down_factors, adapter_weights):
        rows, width = pretrained_weight.shape
        whole_blocks = width % (nr * QB) == 0 and rows % CHUNK == 0 and nc % 2 == 0
        if whole_blocks and up_factors.shape[1] % QB == 0:
            return serving_shards(nr, nc, pretrained_weight, up_factors, down_factors, adapter_weights)
        return panel_shards(pretrained_weight, up_factors, down_factors, adapter_weights)

    return jax.shard_map(
        shards,
        mesh=mesh,
        in_specs=(P("row", "col"), P("row", "col"), P("row", "col"), P()),
        out_specs=(P(None, ("col", "row")), P("row", "col")),
        check_vma=False,
    )
```

time: 1020 us -> 525 us (0.51)
  waiting for transfers between devices: 797 us -> 0 us
  Pallas kernels: 0 us -> 507 us
  local copies, waits for them, and re-layouts: 117 us -> 15.1 us
  matrix products: 42.3 us -> 0 us
  other arithmetic: 39.8 us -> 1.94 us
  between operations: 14.1 us -> 0.66 us
    pallas_call x0 -> x1, Pallas kernels: none -> 507 us  [merge(): pl.pallas_call(functools.partial(merge_kernel, nr, nc), out_shape=[jax.Sh...]
    all_gather x2 -> x0, waiting for transfers between devices: 501 us -> none  [the longest x1 461 us: shards(): lax.all_gather(down_factors, 'row', axis=0, tiled=True)]
    all_to_all x1 -> x0, waiting for transfers between devices: 295 us -> none  [shards(): lax.all_to_all(values, 'row', split_axis=1, concat_axis=0, tiled=True)]
    dot_general x1 -> x0, matrix products: 42.3 us -> none  [shards(): jnp.dot(b_panel, lax.all_gather(down_factors, 'row', axis=0, tiled=True),...]
    div x2 -> x0, local copies, waits for them, and re-layouts: 36.4 us -> none  [scale_tiles(): tiles / largest[:, None, :, None]]
    abs x1 -> x0, local copies, waits for them, and re-layouts: 29.6 us -> none  [scale_tiles(): largest = jnp.max(jnp.abs(tiles), axis=(1, 3)) + 1e-06]
    convert_element_type x2 -> x1, other arithmetic: 28.5 us -> 1.94 us  [weighted_factors(): (up_factors.astype(jnp.float32) * local_scale[None, :]).astype(jnp.bfloat16)]
    unnamed x4 -> x1, local copies, waits for them, and re-layouts: 38 us -> 12.4 us
  transfers between devices with their start and end apart: 3 -> 0, of which waited for: 3 -> 0; matrix products, arithmetic and copies ran while one was open for 0% -> 0% of each run, Pallas kernels for 0% -> 0%
where the time goes in v1:
time: 525 us
  Pallas kernels  507 us (97%)
  local copies, waits for them, and re-layouts  15.1 us (3%)
    pallas_call x1, Pallas kernels, merge(): pl.pallas_call(functools.partial(merge_kernel, nr, nc), out_shape=[jax.Sh...  507 us
    unnamed x1, local copies, waits for them, and re-layouts  12.4 us

profile of v1, /device:TPU:0, one launch (start us, length us, event | category | flops | bytes accessed | tf_op | source)
XLA Modules:
  0.0 525.1 jit_solution(11220750561792606948)
XLA Ops:
  0.6 0.7 broadcast_in_dim.4
  1.4 0.1 reshape.11
  1.4 0.1 dynamic_slice.3
  1.5 1.9 multiply_convert_fusion.b_in
  3.4 507.5 %shard_map.59 = (bf16[4096,1664]{1,0:T(8,128)(2,1)}, f32[4,8,13,128]{3,2,1,0:T(8,128)}) custom-call(bf16[1024,256]{1,0:T(8,128)(2,1)} %multiply_convert_fusion.b_in, bf16[512,6656]{1,0:T(8,128)(2,1)} %a_in.1, bf16[1024,6656]{1,0:T(8,128)(2,1)} %w_in.1), custom_call_target="tpu_custom_call" | custom-call | flops 27917287424 | bytes 27262976 | tf_op jit(solution)/shard_map/pallas_call | solution.py:240
  510.9 1.1 slice_reduce_fusion
  512.0 0.7 reshape.12
  512.7 12.4 %copy.8 = bf16[4096,1664]{1,0:T(8,128)(2,1)} copy(bf16[4096,1664]{1,0:T(8,128)(2,1)} %get-tuple-element.8) | data formatting | bytes 27262976
  (1 shorter events, 0.0 us)

commit v2 on v1

v2 whole, which is shorter than its diff:
```python
import functools

import jax
import jax.numpy as jnp
from jax import lax
from jax.experimental import pallas as pl
from jax.experimental.pallas import tpu as pltpu
from jax.sharding import PartitionSpec as P

RANK = 64
QB = 128
CHUNK = 256


def weighted_factors(up_factors, adapter_weights):
    local_rank_slab = up_factors.shape[1]
    broadcast_scales = jnp.repeat(adapter_weights, RANK)
    offset = lax.axis_index("col") * local_rank_slab
    local_scale = lax.dynamic_slice_in_dim(broadcast_scales, offset, local_rank_slab, 0)
    return (up_factors.astype(jnp.float32) * local_scale[None, :]).astype(jnp.bfloat16)


def scale_tiles(merged_weight):
    row_count, col_count = merged_weight.shape
    tiles = merged_weight.reshape(row_count // QB, QB, col_count // QB, QB)
    largest = jnp.max(jnp.abs(tiles), axis=(1, 3)) + 1e-06
    values = (tiles / largest[:, None, :, None]).astype(jnp.bfloat16).reshape(row_count, col_count)
    return (values, largest)


def panel_shards(pretrained_weight, up_factors, down_factors, adapter_weights):
    weighted_update = weighted_factors(up_factors, adapter_weights)
    b_panel = lax.all_gather(weighted_update, "col", axis=1, tiled=True)
    merged_weight = pretrained_weight.astype(jnp.float32) + jnp.dot(
        b_panel,
        lax.all_gather(down_factors, "row", axis=0, tiled=True),
        preferred_element_type=jnp.float32,
    )
    values, largest = scale_tiles(merged_weight)
    serving = lax.all_to_all(values, "row", split_axis=1, concat_axis=0, tiled=True)
    return (serving, largest)


def merge_kernel(
    nr, nc, s_in, b_in, a_in, w_in, w_full, scales_out,
    a_full, b_raw, b_full, s_own, s_all,
    a_send, a_recv, b_send, b_recv, line_send, w_send, w_recv, s_send, s_recv, local_sem,
):
    rows, width = w_in.shape
    cols = width // nr
    depth = a_in.shape[0]
    planes = nc // 2
    chunks = rows // CHUNK
    per_chunk = CHUNK // QB
    blocks = cols // QB
    r = lax.axis_index("row")
    c = lax.axis_index("col")
    chip, core = c // 2, lax.rem(c, 2)
    sibling = chip * 2 + (1 - core)

    def z_peer(i):
        return lax.rem(r + i, nr)

    def plane_peer(i):
        return lax.rem(chip + i, planes) * 2 + core

    barrier = pltpu.get_barrier_semaphore()
    for i in range(1, nr):
        pl.semaphore_signal(barrier, inc=1, device_id={"row": z_peer(i)}, device_id_type=pl.DeviceIdType.MESH)
    for i in range(1, planes):
        pl.semaphore_signal(barrier, inc=1, device_id={"col": plane_peer(i)}, device_id_type=pl.DeviceIdType.MESH)
    pl.semaphore_signal(barrier, inc=1, device_id={"col": sibling}, device_id_type=pl.DeviceIdType.MESH)
    pl.semaphore_wait(barrier, nr - 1 + planes - 1 + 1)

    def columns(j):
        return pl.ds(pl.multiple_of(j * cols, QB), cols)

    def b_slot(j, q):
        return b_full.at[q, pl.ds(j * rows, rows), :]

    half = nr // 2
    own_half = r // half * half
    gate = jnp.where(own_half == 0, half, half - 1)
    inner = jnp.where(own_half == 0, half - 1, half)

    def mate(m):
        return own_half + lax.rem(r - own_half + m, half)

    def b_plane(j, to):
        return pltpu.make_async_remote_copy(
            src_ref=b_slot(j, c), dst_ref=b_slot(j, c), send_sem=line_send.at[j, to], recv_sem=b_recv.at[j, c],
            device_id={"row": to}, device_id_type=pl.DeviceIdType.MESH)

    load = pltpu.make_async_copy(b_in, b_raw, local_sem.at[1])
    load.start()
    own_a = pltpu.make_async_copy(a_in.at[:, columns(r)], a_full.at[pl.ds(r * depth, depth), :], local_sem.at[0])
    own_a.start()
    own_w = pltpu.make_async_copy(w_in.at[:, columns(r)], w_full.at[pl.ds(r * rows, rows), :], local_sem.at[2])
    own_w.start()
    ranks = b_in.shape[1]
    lane = lax.broadcasted_iota(jnp.int32, (1, ranks), 1)
    weights = jnp.zeros((1, ranks), jnp.float32)
    for k in range(ranks // RANK):
        here = (lane >= k * RANK) & (lane < (k + 1) * RANK)
        weights = jnp.where(here, s_in[c * (ranks // RANK) + k], weights)
    load.wait()

    @pl.loop(0, rows // QB)
    def _(y):
        from_row = pl.multiple_of(y * QB, QB)
        b_full[c, pl.ds(pl.multiple_of(r * rows + y * QB, QB), QB), :] = (
            b_raw[pl.ds(from_row, QB), :].astype(jnp.float32) * weights).astype(jnp.bfloat16)

    b_plane(r, gate).start()
    for m in range(1, half):
        b_plane(r, mate(m)).start()

    for i in range(1, nr):
        pltpu.make_async_remote_copy(
            src_ref=a_in.at[:, columns(z_peer(i))], dst_ref=a_full.at[pl.ds(r * depth, depth), :],
            send_sem=a_send.at[i], recv_sem=a_recv.at[r],
            device_id={"row": z_peer(i)}, device_id_type=pl.DeviceIdType.MESH).start()
    def w_copy(i, t):
        source = pl.multiple_of(t * CHUNK, CHUNK)
        return pltpu.make_async_remote_copy(
            src_ref=w_in.at[pl.ds(source, CHUNK), columns(z_peer(i))],
            dst_ref=w_full.at[pl.ds(pl.multiple_of(r * rows + t * CHUNK, CHUNK), CHUNK), :],
            send_sem=w_send.at[i, t], recv_sem=w_recv.at[r, t],
            device_id={"row": z_peer(i)}, device_id_type=pl.DeviceIdType.MESH)

    def b_wait(j, q):
        slot = b_slot(j, q)
        pltpu.make_async_copy(slot, slot, b_recv.at[j, q]).wait()

    def b_share(k, j, q, to, src):
        return pltpu.make_async_remote_copy(
            src_ref=src, dst_ref=b_slot(j, q), send_sem=b_send.at[k[0], k[1]], recv_sem=b_recv.at[j, q],
            device_id={"col": to}, device_id_type=pl.DeviceIdType.MESH)

    for i in range(1, nr):
        w_copy(i, 0).start()

    def spread(j):
        for i in range(1, planes):
            b_share((j, i), j, c, plane_peer(i), b_slot(j, c)).start()
        b_share((j, planes), j, c, sibling, b_slot(j, c)).start()

    spread(r)
    for m in range(1, half):
        b_wait(mate(m), c)
        spread(mate(m))
    for m in range(half):
        j = half - own_half + m
        b_wait(j, c)

        @pl.when(r == inner)
        def _(j=j):
            for k in range(1, half):
                b_plane(j, mate(k)).start()

        spread(j)

    @pl.loop(0, nr)
    def _(j):
        for i in range(1, planes):
            q = plane_peer(i)
            b_wait(j, q)
            b_share((j, planes + i), j, q, sibling, b_slot(j, q)).start()

    @pl.loop(1, chunks)
    def _(t):
        for i in range(1, nr):
            w_copy(i, t).start()

    @pl.loop(0, nr)
    def _(j):
        for i in range(planes):
            b_wait(j, lax.rem(chip + i, planes) * 2 + (1 - core))

    own_a.wait()
    for i in range(1, nr):
        part = a_full.at[pl.ds(z_peer(i) * depth, depth), :]
        pltpu.make_async_copy(part, part, a_recv.at[z_peer(i)]).wait()

    def merge_cols(j, t, col, count):
        row = pl.multiple_of(j * rows + t * CHUNK, CHUNK)
        at = pl.ds(row, CHUNK)
        lhs = jnp.concatenate([b_full[q, at, :] for q in range(nc)], axis=1)
        part = pl.ds(pl.multiple_of(col * QB, QB), count * QB)
        merged = w_full[at, part].astype(jnp.float32) + jnp.dot(
            lhs, a_full[:, part], preferred_element_type=jnp.float32)
        for y in range(per_chunk):
            for x in range(count):
                tile = merged[y * QB:(y + 1) * QB, x * QB:(x + 1) * QB]
                largest = jnp.max(jnp.max(jnp.abs(tile), axis=0, keepdims=True), axis=1, keepdims=True) + 1e-06
                w_full[pl.ds(pl.multiple_of(row + y * QB, QB), QB), pl.ds(pl.multiple_of((col + x) * QB, QB), QB)] = (
                    tile / largest).astype(jnp.bfloat16)
                s_own[j, t * per_chunk + y, pl.ds(col + x, 1), :] = jnp.broadcast_to(largest, (1, QB))

    def merge_chunk(j, t):
        @pl.loop(0, blocks // 2)
        def _(pair):
            merge_cols(j, t, pair * 2, 2)

        if blocks % 2:
            merge_cols(j, t, blocks - 1, 1)

    own_w.wait()

    @pl.loop(0, chunks)
    def _(t):
        merge_chunk(r, t)

    @pl.loop(0, chunks * (nr - 1))
    def _(n):
        t = n // (nr - 1)
        j = lax.rem(r + 1 + lax.rem(n, nr - 1), nr)
        part = w_full.at[pl.ds(pl.multiple_of(j * rows + t * CHUNK, CHUNK), CHUNK), :]
        pltpu.make_async_copy(part, part, w_recv.at[j, t]).wait()
        merge_chunk(j, t)

    def s_copy(i):
        return pltpu.make_async_remote_copy(
            src_ref=s_own.at[z_peer(i)], dst_ref=s_all.at[r], send_sem=s_send.at[i], recv_sem=s_recv.at[r],
            device_id={"row": z_peer(i)}, device_id_type=pl.DeviceIdType.MESH)

    for i in range(1, nr):
        s_copy(i).start()
    s_all[r] = s_own[r]
    for i in range(1, nr):
        pltpu.make_async_copy(s_own.at[0], s_all.at[z_peer(i)], s_recv.at[z_peer(i)]).wait()
    to_out = pltpu.make_async_copy(s_all, scales_out, local_sem.at[3])
    to_out.start()

    for i in range(1, nr):
        s_copy(i).wait_send()
        part = a_full.at[pl.ds(r * depth, depth), :]
        pltpu.make_async_copy(part, part, a_send.at[i]).wait()

    @pl.loop(0, nr)
    def _(j):
        for k in range(1, 2 * planes):
            pltpu.make_async_copy(b_in, b_in, b_send.at[j, k]).wait()

    b_plane(r, gate).wait_send()
    for m in range(1, half):
        b_plane(r, mate(m)).wait_send()

    @pl.when(r == inner)
    def _():
        for m in range(half):
            for k in range(1, half):
                b_plane(half - own_half + m, mate(k)).wait_send()

    @pl.loop(0, chunks)
    def _(t):
        for i in range(1, nr):
            w_copy(i, t).wait_send()

    to_out.wait()


def merge(nr, nc, adapter_weights, b, a, w):
    rows, width = w.shape
    cols = width // nr
    depth = a.shape[0]
    chunks = rows // CHUNK
    blocks = cols // QB
    dma = pltpu.SemaphoreType.DMA
    return pl.pallas_call(
        functools.partial(merge_kernel, nr, nc),
        out_shape=[
            jax.ShapeDtypeStruct((nr * rows, cols), jnp.bfloat16),
            jax.ShapeDtypeStruct((nr, rows // QB, blocks, QB), jnp.float32),
        ],
        in_specs=[pl.BlockSpec(memory_space=pltpu.SMEM)] + [pl.BlockSpec(memory_space=pltpu.HBM)] * 3,
        out_specs=[pl.BlockSpec(memory_space=pltpu.VMEM), pl.BlockSpec(memory_space=pltpu.HBM)],
        scratch_shapes=[
            pltpu.VMEM((nr * depth, cols), jnp.bfloat16),
            pltpu.VMEM(b.shape, jnp.bfloat16),
            pltpu.VMEM((nc, nr * rows, b.shape[1]), jnp.bfloat16),
            pltpu.VMEM((nr, rows // QB, blocks, QB), jnp.float32),
            pltpu.VMEM((nr, rows // QB, blocks, QB), jnp.float32),
            dma((nr,)), dma((nr,)),
            dma((nr, nc)), dma((nr, nc)), dma((nr, nr)),
            dma((nr, chunks)), dma((nr, chunks)),
            dma((nr,)), dma((nr,)),
            dma((4,)),
        ],
        compiler_params=pltpu.CompilerParams(
            collective_id=0, has_side_effects=True, vmem_limit_bytes=32 * 2 ** 20),
        cost_estimate=pl.CostEstimate(
            flops=2 * nr * rows * nr * depth * cols, bytes_accessed=4 * rows * width, transcendentals=0),
    )(adapter_weights, b, a, w)


def store_kernel(parts, values, out, sem):
    count = values.shape[0] // parts
    copies = [
        pltpu.make_async_copy(values.at[pl.ds(i * count, count), :], out.at[pl.ds(i * count, count), :], sem.at[i])
        for i in range(parts)
    ]
    for copy in copies:
        copy.start()
    for copy in copies:
        copy.wait()


def store(values, parts):
    return pl.pallas_call(
        functools.partial(store_kernel, parts),
        out_shape=jax.ShapeDtypeStruct(values.shape, values.dtype),
        in_specs=[pl.BlockSpec(memory_space=pltpu.VMEM)],
        out_specs=pl.BlockSpec(memory_space=pltpu.HBM),
        scratch_shapes=[pltpu.SemaphoreType.DMA((parts,))],
        compiler_params=pltpu.CompilerParams(vmem_limit_bytes=2 ** 20),
    )(values)


def serving_shards(nr, nc, pretrained_weight, up_factors, down_factors, adapter_weights):
    values, scales = merge(nr, nc, adapter_weights, up_factors, down_factors, pretrained_weight)
    largest = jnp.transpose(scales[:, :, :, 0], (1, 0, 2)).reshape(scales.shape[1], -1)
    return (store(values, 8), largest)


def solution(mesh):
    nr, nc = mesh.shape["row"], mesh.shape["col"]

    def shards(pretrained_weight, up_factors, down_factors, adapter_weights):
        rows, width = pretrained_weight.shape
        whole_blocks = width % (nr * QB) == 0 and rows % CHUNK == 0 and nc % 2 == 0 and nr % 2 == 0
        if whole_blocks and up_factors.shape[1] % QB == 0:
            return serving_shards(nr, nc, pretrained_weight, up_factors, down_factors, adapter_weights)
        return panel_shards(pretrained_weight, up_factors, down_factors, adapter_weights)

    return jax.shard_map(
        shards,
        mesh=mesh,
        in_specs=(P("row", "col"), P("row", "col"), P("row", "col"), P()),
        out_specs=(P(None, ("col", "row")), P("row", "col")),
        check_vma=False,
    )
```

time: 525 us -> 496 us (0.945)
  Pallas kernels: 507 us -> 490 us
  local copies, waits for them, and re-layouts: 15.1 us -> 5.44 us
    pallas_call x1, Pallas kernels: 507 us -> 485 us  [merge(): pl.pallas_call(functools.partial(merge_kernel, nr, nc), out_shape=[jax.Sh...]
    unnamed x1 -> x6, local copies, waits for them, and re-layouts: 12.4 us -> 4.62 us
where the time goes in v2:
time: 496 us
  Pallas kernels  490 us (99%)
  local copies, waits for them, and re-layouts  5.44 us (1%)
    pallas_call x1, Pallas kernels, merge(): pl.pallas_call(functools.partial(merge_kernel, nr, nc), out_shape=[jax.Sh...  485 us

profile of v2, /device:TPU:0, one launch (start us, length us, event | category | flops | bytes accessed | tf_op | source)
XLA Modules:
  0.0 496.1 jit_solution(10526271151386782919)
XLA Ops:
  0.6 0.0 copy-start
  0.6 2.9 copy-done
  3.6 0.0 copy-start.1
  3.6 1.0 copy-done.1
  4.6 0.0 copy-start.2
  4.6 0.7 copy-done.2
  5.3 485.0 %shard_map.59 = (bf16[4096,1664]{1,0:T(8,128)(2,1)S(1)}, f32[4,8,13,128]{3,2,1,0:T(8,128)S(1)}) custom-call(f32[32]{0:T(128)S(1)} %copy-done.2, bf16[1024,256]{1,0:T(8,128)(2,1)S(1)} %copy-done.1, bf16[512,6656]{1,0:T(8,128)(2,1)S(1)} %copy-done, bf16[1024,6656]{1,0:T(8,128)(2,1)} %w_in.1), custom_call_target="tpu_custom_call" | custom-call | flops 27917287424 | bytes 27262976 | tf_op jit(solution)/shard_map/pallas_call | solution.py:270
  490.3 5.0 %shard_map.60 = bf16[4096,1664]{1,0:T(8,128)(2,1)} custom-call(bf16[4096,1664]{1,0:T(8,128)(2,1)S(1)} %get-tuple-element.4.values), custom_call_target="tpu_custom_call" | custom-call | tf_op jit(solution)/shard_map/pallas_call | solution.py:310
  495.3 0.1 slice_reduce_fusion
  495.4 0.7 reshape.7
  (1 shorter events, 0.0 us)
Async XLA Ops:
  0.6 2.9 copy-start
  3.6 1.0 copy-start.1
  4.6 0.7 copy-start.2

commit v3 on v2

--- a/solution.py
+++ b/solution.py
@@ -9,7 +9,7 @@
 
 RANK = 64
 QB = 128
-CHUNK = 256
+CHUNK = 128
 
 
 def weighted_factors(up_factors, adapter_weights):

time: 496 us -> 494 us (level)
  no operation moved by 1% of the time
where the time goes in v3:
time: 494 us
  Pallas kernels  488 us (99%)
  local copies, waits for them, and re-layouts  5.44 us (1%)
    pallas_call x1, Pallas kernels, merge(): pl.pallas_call(functools.partial(merge_kernel, nr, nc), out_shape=[jax.Sh...  483 us

profile of v3, /device:TPU:0, one launch (start us, length us, event | category | flops | bytes accessed | tf_op | source)
XLA Modules:
  0.0 493.9 jit_solution(14064821496832212416)
XLA Ops:
  0.6 0.0 copy-start
  0.6 2.9 copy-done
  3.6 0.0 copy-start.1
  3.6 1.0 copy-done.1
  4.6 0.0 copy-start.2
  4.6 0.7 copy-done.2
  5.3 482.8 %shard_map.59 = (bf16[4096,1664]{1,0:T(8,128)(2,1)S(1)}, f32[4,8,13,128]{3,2,1,0:T(8,128)S(1)}) custom-call(f32[32]{0:T(128)S(1)} %copy-done.2, bf16[1024,256]{1,0:T(8,128)(2,1)S(1)} %copy-done.1, bf16[512,6656]{1,0:T(8,128)(2,1)S(1)} %copy-done, bf16[1024,6656]{1,0:T(8,128)(2,1)} %w_in.1), custom_call_target="tpu_custom_call" | custom-call | flops 27917287424 | bytes 27262976 | tf_op jit(solution)/shard_map/pallas_call | solution.py:270
  488.1 5.0 %shard_map.60 = bf16[4096,1664]{1,0:T(8,128)(2,1)} custom-call(bf16[4096,1664]{1,0:T(8,128)(2,1)S(1)} %get-tuple-element.4.values), custom_call_target="tpu_custom_call" | custom-call | tf_op jit(solution)/shard_map/pallas_call | solution.py:310
  493.1 0.1 slice_reduce_fusion
  493.2 0.7 reshape.7
  (1 shorter events, 0.0 us)
Async XLA Ops:
  0.6 2.9 copy-start
  3.6 1.0 copy-start.1
  4.6 0.7 copy-start.2
